TPU v7x, 32 devices: a whole 2x2x4 slice. The times are simulated.
32 devices in a mesh: groups: 2 (over y), dp: 4 (over z), feat: 4 (over x, core).
Axes of the slice: x: 2, y: 2, z: 4, core: 2. Of those that a mesh axis runs over, the one named last changes fastest.
Arguments:
- train_feats: bfloat16 [4096, 8192], P('dp', 'feat'), may hold values from -6 to 6
- pool_feats: bfloat16 [64, 8192], P('dp', 'feat'), may hold values from -6 to 6
- kernel_inv: bfloat16 [8192, 8192], P('feat', 'dp')
- test_ids: int32 [384], P('groups'), parts along dimension 0, may hold values from 0 to 63
Outputs:
- scores: bfloat16 [4096, 384], P(('dp', 'feat'), 'groups'), parts along dimension 1
There are 2 independent parts, one for each index of `groups`. A program takes and returns all parts, laid end to end along the dimension named above; an argument that names none is the same for every part. Nothing has to cross between parts.
All inputs are finite; a program needn't handle non-finite values.
Results may differ from a plain program's by a relative error of at most 0.0051.
Values may be sent and summed in bfloat16 or wider, within the bound.
A program may use at most 64 MiB of HBM per device.

v0:
```python
import jax
import jax.numpy as jnp
from jax import lax
from jax.sharding import PartitionSpec as P


def per_device(train_feats, pool_feats, kernel_inv, test_ids):
    feat_width = train_feats.shape[1]
    whole_pool = lax.all_gather(pool_feats, "dp", axis=0, tiled=True)
    test_rows = jnp.take(whole_pool, test_ids, axis=0)
    partial_value = jnp.dot(test_rows, kernel_inv, preferred_element_type=jnp.float32)
    summed = lax.psum(partial_value, "feat").astype(jnp.bfloat16)
    every_col = lax.all_gather(summed, "dp", axis=1, tiled=True)
    start = lax.axis_index("feat") * feat_width
    precond = lax.dynamic_slice_in_dim(every_col, start, feat_width, 1)
    terms = lax.dot_general(
        train_feats, precond, (((1,), (1,)), ((), ())), preferred_element_type=jnp.float32
    )
    mine = lax.psum_scatter(terms, "feat", scatter_dimension=0, tiled=True)
    return mine.astype(jnp.bfloat16)


def solution(mesh):
    placed = (P("dp", "feat"), P("dp", "feat"), P("feat", "dp"), P("groups"))
    return jax.shard_map(
        per_device,
        mesh=mesh,
        in_specs=placed,
        out_specs=P(("dp", "feat"), "groups"),
        check_vma=False,
    )
```

profile of v0, /device:TPU:0, one launch (start us, length us, event | category | flops | bytes accessed | tf_op | source)
XLA Modules:
  0.0 162.8 jit_solution(8902812452308058284)
XLA Ops:
  6.5 0.0 all-gather.2.cloned.1.call-start
  6.5 0.7 compare_select_fusion
  7.2 0.7 compare_and_fusion
  7.9 15.8 %all_gather.6 = bf16[64,2048]{1,0:T(8,128)(2,1)S(1)} all-gather(bf16[16,2048]{1,0:T(8,128)(2,1)} %param.5), channel_id=1, replica_groups=mesh['groups'=2,'dp'=4,'feat'=4] {'dp'}, dimensions={0}, use_global_device_ids=true | all-gather | bytes 327680 | tf_op jit(solution)/shard_map/all_gather | solution.py:9
  23.7 1.1 gather_fusion
  24.9 5.2 %fusion.1 = f32[192,2048]{1,0:T(8,128)S(1)} fusion(bf16[2048,2048]{1,0:T(8,128)(2,1)} %param.6, bf16[192,2048]{1,0:T(8,128)(2,1)S(1)} %gather_fusion, pred[192]{0:T(512)(128)(4,1)S(1)} %compare_and_fusion), kind=kOutput, calls=%fused_computation.3 | convolution fusion | flops 1611005952 | bytes 10748096 | tf_op jit(solution)/shard_map/dot_general | solution.py:11
  30.1 32.8 %all-reduce.1 = bf16[192,2048]{1,0:T(8,128)(2,1)} all-reduce(f32[192,2048]{1,0:T(8,128)S(1)} %fusion.1), channel_id=1, replica_groups=mesh['groups'=2,'dp'=4,'feat'=4] {'feat'}, use_global_device_ids=true, to_apply=%region_0.1 | all-reduce | flops 393216 | bytes 2359296 | tf_op jit(solution)/shard_map/psum | solution.py:12
  62.9 0.0 all-gather.2.cloned.1.call-update
  63.0 0.0 reduce-scatter.2.cloned.1.call-start
  63.0 64.4 %all-gather.2.cloned.1.call-done = bf16[192,8192]{1,0:T(8,128)(2,1)} async-done(((bf16[192,2048]{1,0:T(8,128)(2,1)}), bf16[192,8192]{1,0:T(8,128)(2,1)}) %all-gather.2.cloned.1.call-update) | async-done | bytes 3145744 | tf_op jit(solution)/shard_map/all_gather | solution.py:13
  127.5 4.8 %convolution_bitcast_fusion = f32[1024,192]{0,1:T(8,128)} fusion(bf16[1024,2048]{1,0:T(8,128)(2,1)} %param.4, bf16[192,8192]{1,0:T(8,128)(2,1)} %all-gather.2.cloned.1.call-done, s32[]{:T(128)S(6)} %select_n.14), kind=kOutput, calls=%fused_computation.1 | convolution fusion | flops 805306368 | bytes 5767172 | tf_op jit(solution)/shard_map/dot_general | solution.py:16
  132.3 0.0 reduce-scatter.2.cloned.1.call-update
  132.3 22.1 %reduce-scatter.2.cloned.1.call-done = f32[256,192]{0,1:T(8,128)} async-done(((f32[1024,192]{0,1:T(8,128)}), f32[256,192]{0,1:T(8,128)}) %reduce-scatter.2.cloned.1.call-update) | async-done | bytes 196624 | tf_op jit(solution)/shard_map/reduce_scatter | solution.py:19
  154.4 1.6 convert_element_type.7
  (1 shorter events, 0.0 us)
Async XLA Ops:
  6.5 120.9 %all-gather.2.cloned.1.call-start = ((), (), s32[]{:S(2)}) async-start(), calls=%async_computation.1 | async-start | bytes 3932160 | tf_op jit(solution)/shard_map/all_gather | solution.py:13
  63.0 91.5 %reduce-scatter.2.cloned.1.call-start = ((), (), s32[]{:S(2)}) async-start(), calls=%async_computation.2 | async-start | bytes 983040 | tf_op jit(solution)/shard_map/reduce_scatter | solution.py:19
Sparse Core Ops, SparseCore 0:
  63.1 64.3 all-gather.1
  132.4 21.9 reduce-scatter.1
where the time goes:
time: 163 us
  waiting for transfers between devices  86.6 us (53%)
  blocking collectives  48.6 us (30%)
  between operations  13.4 us (8%)
  matrix products  10.1 us (6%)
  other arithmetic  2.95 us (2%)
    all_gather x1, waiting for transfers between devices, per_device(): every_col = lax.all_gather(summed, 'dp', axis=1, tiled=True)  64.4 us
    psum x1, blocking collectives, per_device(): summed = lax.psum(partial_value, 'feat').astype(jnp.bfloat16)  32.8 us
    reduce_scatter x1, waiting for transfers between devices, per_device(): mine = lax.psum_scatter(terms, 'feat', scatter_dimension=0, tiled=True)  22.1 us
    all_gather x1, blocking collectives, per_device(): whole_pool = lax.all_gather(pool_feats, 'dp', axis=0, tiled=True)  15.8 us
    dot_general x1, matrix products, per_device(): jnp.dot(test_rows, kernel_inv, preferred_element_type=jnp.float32)  5.24 us
    dot_general x1, matrix products, per_device(): lax.dot_general(train_feats, precond, (((1,), (1,)), ((), ())), preferred...  4.85 us
  transfers between devices with their start and end apart: 2, of which 2 were waited for; matrix products, arithmetic and copies ran while one was open for 0% of the time, Pallas kernels for 0%

commit v1 on v0

v1 whole, which is shorter than its diff:
```python
import functools

import jax
import jax.numpy as jnp
from jax import lax
from jax.experimental import pallas as pl
from jax.experimental.pallas import tpu as pltpu
from jax.sharding import PartitionSpec as P

MESH = pl.DeviceIdType.MESH
F32 = jnp.float32
BF16 = jnp.bfloat16
NT = (((1,), (1,)), ((), ()))
TN = (((0,), (0,)), ((), ()))


def per_device(train_feats, pool_feats, kernel_inv, test_ids):
    feat_width = train_feats.shape[1]
    whole_pool = lax.all_gather(pool_feats, "dp", axis=0, tiled=True)
    test_rows = jnp.take(whole_pool, test_ids, axis=0)
    partial_value = jnp.dot(test_rows, kernel_inv, preferred_element_type=F32)
    summed = lax.psum(partial_value, "feat").astype(BF16)
    every_col = lax.all_gather(summed, "dp", axis=1, tiled=True)
    start = lax.axis_index("feat") * feat_width
    precond = lax.dynamic_slice_in_dim(every_col, start, feat_width, 1)
    terms = lax.dot_general(train_feats, precond, NT, preferred_element_type=F32)
    mine = lax.psum_scatter(terms, "feat", scatter_dimension=0, tiled=True)
    return mine.astype(BF16)


def pick_columns(scores, ids, pool):
    rounded = scores.astype(BF16).astype(F32)
    finite = jnp.abs(rounded) <= float(jnp.finfo(BF16).max)
    value = jnp.where(finite, rounded, 0.0).astype(BF16)
    code = jnp.where(finite, 0.0, jnp.where(rounded > 0, 1.0, jnp.where(rounded < 0, 2.0, 3.0))).astype(BF16)
    places = lax.broadcasted_iota(jnp.int32, (pool, ids.shape[1]), 0)
    chosen = jnp.where(places == ids, 1.0, 0.0).astype(BF16)
    picked = lax.dot_general(value, chosen, TN, preferred_element_type=F32)
    codes = lax.dot_general(code, chosen, TN, preferred_element_type=F32)
    special = jnp.where(codes == 1.0, jnp.inf, jnp.where(codes == 2.0, -jnp.inf, jnp.nan))
    return jnp.where(codes == 0.0, picked, special).astype(BF16)


def kernel(
    train_hbm, pool_hbm, kinv_hbm, ids_hbm, out_ref,
    kinv, train, ids, pool, part1, got1, part2, got2, slices, precond, part3, got3, part4, got4,
    load_sem, pool_send, pool_recv, send1, recv1, send2, recv2, send3, recv3, send4, recv4, send5, recv5, send6, recv6,
):
    g, d, f = lax.axis_index("groups"), lax.axis_index("dp"), lax.axis_index("feat")
    x, c = f // 2, f % 2
    depth, width = kinv.shape[1], kinv.shape[2]
    pool_rows = pool.shape[0] * pool.shape[1]
    sibling = (g, d, 2 * x + 1 - c)
    around = [(1 - g, 1 - x), (1 - g, x), (g, 1 - x), (g, x)]
    me = c * 4 + g * 2 + x

    def remote(src, dst, send, recv, device):
        return pltpu.make_async_remote_copy(
            src_ref=src, dst_ref=dst, send_sem=send, recv_sem=recv, device_id=device, device_id_type=MESH
        )

    loads = []

    def load(src, dst):
        copy = pltpu.make_async_copy(src, dst, load_sem.at[len(loads)])
        copy.start()
        loads.append(copy)
        return copy

    depth_from = pl.multiple_of(g * depth, depth)
    pool_half = pool_hbm.at[:, pl.ds(depth_from, depth)]
    own_pool = load(pool_half, pool.at[d])
    kinv_loads = []
    for i in range(8):
        core = 1 - c if i < 4 else c
        gg, xx = around[i % 4]
        col = pl.multiple_of((core * 4 + gg * 2 + xx) * width, width)
        kinv_loads.append(load(kinv_hbm.at[pl.ds(depth_from, depth), pl.ds(col, width)], kinv.at[i]))
    train_loads = [
        load(train_hbm.at[pl.ds(i * train.shape[1], train.shape[1]), :], train.at[i]) for i in range(4)
    ]
    ids_load = load(ids_hbm, ids)

    barrier = pltpu.get_barrier_semaphore()
    for r in range(1, 4):
        pl.semaphore_signal(barrier, inc=1, device_id=(g, (d + r) % 4, f), device_id_type=MESH)
    for r in range(4):
        for gg in (g, 1 - g) if r else (1 - g,):
            pl.semaphore_signal(barrier, inc=1, device_id=(gg, d, (f + r) % 4), device_id_type=MESH)
    pl.semaphore_wait(barrier, 10)

    sends = []

    pool_copies = []
    for r in range(1, 4):
        copy = remote(pool_half, pool.at[d], pool_send.at[r], pool_recv.at[r], (g, (d + r) % 4, f))
        copy.start()
        pool_copies.append(copy)
    own_pool.wait()
    for copy in pool_copies:
        copy.wait_recv()
    rows = pool[...].reshape(pool_rows, depth)

    copies1 = []
    for i in range(4):
        kinv_loads[i].wait()
        part1[i] = jnp.dot(rows, kinv[i], preferred_element_type=F32)
        copy = remote(part1.at[i], got1.at[i], send1.at[i], recv1.at[i], sibling)
        copy.start()
        copies1.append(copy)
    copies2 = []
    for i in range(4):
        kinv_loads[4 + i].wait()
        term = jnp.dot(rows, kinv[4 + i], preferred_element_type=F32)
        copies1[i].wait_recv()
        part2[i] = term + got1[i]
        if i < 3:
            gg, xx = around[i]
            copy = remote(part2.at[i], got2.at[i], send2.at[i], recv2.at[i], (gg, d, 2 * xx + c))
            copy.start()
            copies2.append(copy)
    total = part2[3]
    for i in (2, 1, 0):
        copies2[i].wait_recv()
        total = total + got2[i]
    slices[d] = total.astype(BF16)

    copies3 = []
    for r in range(1, 4):
        copy = remote(slices.at[d], slices.at[d], send3.at[r], recv3.at[r], (g, (d + r) % 4, f))
        copy.start()
        copies3.append(copy)

    col = pl.multiple_of(me * width, width)

    def forward(n, j):
        mine = precond.at[:, pl.ds(col, width)]
        across = remote(slices.at[j], mine, send4.at[n, 1], recv4.at[me], (1 - g, d, j))
        beside = remote(slices.at[j], mine, send4.at[n, 0], recv4.at[me], (g, d, j))
        across.start()

        @pl.when(f != j)
        def _():
            beside.start()

        @pl.when(f == j)
        def _():
            precond[:, pl.ds(col, width)] = slices[j]

        return across, beside, j

    forwards = [forward(0, d)]
    for r in range(1, 4):
        copies3[r - 1].wait_recv()
        forwards.append(forward(r, (d - r + 4) % 4))
    for r in range(1, 8):
        k = (me + r) % 8
        other = precond.at[:, pl.ds(pl.multiple_of(k * width, width), width)]
        pltpu.make_async_remote_copy(
            src_ref=other, dst_ref=other, send_sem=send4.at[0, 0], recv_sem=recv4.at[k],
            device_id=sibling, device_id_type=MESH,
        ).wait_recv()

    for copy in train_loads:
        copy.wait()
    left = precond[...]

    def term(j):
        return lax.dot_general(left, train[j], NT, preferred_element_type=F32)

    copies5 = []
    for i, xx in enumerate((1 - x, x)):
        part3[i] = term(2 * xx + 1 - c)
        copy = remote(part3.at[i], got3.at[i], send5.at[i], recv5.at[i], sibling)
        copy.start()
        copies5.append(copy)
    first = term(2 * (1 - x) + c)
    copies5[0].wait_recv()
    part4[...] = first + got3[0]
    copy6 = remote(part4, got4, send6, recv6, (g, d, 2 * (1 - x) + c))
    copy6.start()
    second = term(f)
    copies5[1].wait_recv()
    second = second + got3[1]
    ids_load.wait()
    copy6.wait_recv()
    out_ref[...] = pick_columns(second + got4[...], ids[...], pool_rows)

    for copy in pool_copies + copies1 + copies2 + copies3 + copies5 + [copy6]:
        copy.wait_send()
    for across, beside, j in forwards:
        across.wait_send()

        @pl.when(f != j)
        def _(beside=beside):
            beside.wait_send()


def fused(train_feats, pool_feats, kernel_inv, test_ids):
    rows, feats = train_feats.shape
    pool_block = pool_feats.shape[0]
    pool_rows = 4 * pool_block
    depth, width = feats // 2, kernel_inv.shape[1] // 8
    out_rows = rows // 4
    queries = test_ids.shape[0]
    dma = pltpu.SemaphoreType.DMA
    return pl.pallas_call(
        kernel,
        out_shape=jax.ShapeDtypeStruct((out_rows, queries), BF16),
        in_specs=[pl.BlockSpec(memory_space=pl.ANY)] * 4,
        out_specs=pl.BlockSpec(memory_space=pltpu.VMEM),
        scratch_shapes=[
            pltpu.VMEM((8, depth, width), BF16),
            pltpu.VMEM((4, out_rows, feats), BF16),
            pltpu.VMEM((1, queries), jnp.int32),
            pltpu.VMEM((4, pool_block, depth), BF16),
            pltpu.VMEM((4, pool_rows, width), F32),
            pltpu.VMEM((4, pool_rows, width), F32),
            pltpu.VMEM((4, pool_rows, width), F32),
            pltpu.VMEM((3, pool_rows, width), F32),
            pltpu.VMEM((4, pool_rows, width), BF16),
            pltpu.VMEM((pool_rows, 8 * width), BF16),
            pltpu.VMEM((2, pool_rows, out_rows), F32),
            pltpu.VMEM((2, pool_rows, out_rows), F32),
            pltpu.VMEM((pool_rows, out_rows), F32),
            pltpu.VMEM((pool_rows, out_rows), F32),
            dma((14,)), dma((4,)), dma((4,)), dma((4,)), dma((4,)), dma((3,)), dma((3,)),
            dma((4,)), dma((4,)), dma((4, 2)), dma((8,)), dma((2,)), dma((2,)), dma, dma,
        ],
        compiler_params=pltpu.CompilerParams(
            collective_id=0, has_side_effects=True, vmem_limit_bytes=48 * 1024 * 1024
        ),
        cost_estimate=pl.CostEstimate(
            flops=2 * pool_rows * feats * (kernel_inv.shape[1] // 2 + rows),
            bytes_accessed=2 * (train_feats.size + kernel_inv.size // 2 + out_rows * queries),
            transcendentals=0,
        ),
    )(train_feats, pool_feats, kernel_inv, test_ids.reshape(1, queries))


def solution(mesh):
    sizes = tuple(mesh.shape[name] for name in ("groups", "dp", "feat"))

    def body(train_feats, pool_feats, kernel_inv, test_ids):
        pool_rows = sizes[1] * pool_feats.shape[0]
        square = train_feats.shape[1] == kernel_inv.shape[1]
        if sizes == (2, 4, 4) and square and pool_rows <= test_ids.shape[0]:
            return fused(train_feats, pool_feats, kernel_inv, test_ids)
        return per_device(train_feats, pool_feats, kernel_inv, test_ids)

    placed = (P("dp", "feat"), P("dp", "feat"), P("feat", "dp"), P("groups"))
    return jax.shard_map(
        body,
        mesh=mesh,
        in_specs=placed,
        out_specs=P(("dp", "feat"), "groups"),
        check_vma=False,
    )
```

time: 163 us -> 37 us (0.23)
  waiting for transfers between devices: 86.6 us -> 0 us
  blocking collectives: 48.6 us -> 0 us
  Pallas kernels: 0 us -> 32.4 us
  between operations: 13.4 us -> 0.01 us
  matrix products: 10.1 us -> 0 us
  local copies, waits for them, and re-layouts: 1.15 us -> 4.45 us
  other arithmetic: 2.95 us -> 0 us
    all_gather x1 -> x0, waiting for transfers between devices: 64.4 us -> none  [per_device(): every_col = lax.all_gather(summed, 'dp', axis=1, tiled=True)]
    psum x1 -> x0, blocking collectives: 32.8 us -> none  [per_device(): summed = lax.psum(partial_value, 'feat').astype(jnp.bfloat16)]
    pallas_call x0 -> x1, Pallas kernels: none -> 32.4 us  [fused(): pl.pallas_call(kernel, out_shape=jax.ShapeDtypeStruct((out_rows, queries)...]
    reduce_scatter x1 -> x0, waiting for transfers between devices: 22.1 us -> none  [per_device(): mine = lax.psum_scatter(terms, 'feat', scatter_dimension=0, tiled=True)]
    all_gather x1 -> x0, blocking collectives: 15.8 us -> none  [per_device(): whole_pool = lax.all_gather(pool_feats, 'dp', axis=0, tiled=True)]
    dot_general x2 -> x0, matrix products: 10.1 us -> none  [the longest x1 5.24 us: per_device(): jnp.dot(test_rows, kernel_inv, preferred_element_type=jnp.float32)]
    unnamed x0 -> x6, local copies, waits for them, and re-layouts: none -> 3.7 us
  transfers between devices with their start and end apart: 2 -> 0, of which waited for: 2 -> 0; matrix products, arithmetic and copies ran while one was open for 0% -> 0% of each run, Pallas kernels for 0% -> 0%
where the time goes in v1:
time: 37 us; the launch traced here: 36.8 us
  Pallas kernels  32.4 us (88%)
  local copies, waits for them, and re-layouts  4.45 us (12%)
    pallas_call x1, Pallas kernels, fused(): pl.pallas_call(kernel, out_shape=jax.ShapeDtypeStruct((out_rows, queries)...  32.4 us
    unnamed x6, local copies, waits for them, and re-layouts  3.7 us
    pallas_call x1, local copies, waits for them, and re-layouts, fused(): pl.pallas_call(kernel, out_shape=jax.ShapeDtypeStruct((out_rows, queries)...  0.75 us

profile of v1, /device:TPU:0, one launch (start us, length us, event | category | flops | bytes accessed | tf_op | source)
XLA Modules:
  0.0 36.8 jit_solution(4033944202238998101)
XLA Ops:
  0.0 0.0 copy-start
  0.0 2.2 %copy-done = bf16[1024,2048]{1,0:T(8,128)(2,1)S(1)} copy-done((bf16[1024,2048]{1,0:T(8,128)(2,1)S(1)}, bf16[1024,2048]{1,0:T(8,128)(2,1)}, u32[]{:S(2)}) %copy-start) | copy-done | bytes 4194328
  2.2 0.0 copy-start.1
  2.2 0.8 %copy-done.1 = bf16[16,2048]{1,0:T(8,128)(2,1)S(1)} copy-done((bf16[16,2048]{1,0:T(8,128)(2,1)S(1)}, bf16[16,2048]{1,0:T(8,128)(2,1)}, u32[]{:S(2)}) %copy-start.1) | copy-done | bytes 65560
  3.0 0.0 copy-start.2
  3.0 0.7 %copy-done.2 = s32[192]{0:T(256)S(1)} copy-done((s32[192]{0:T(256)S(1)}, s32[192]{0:T(256)}, u32[]{:S(2)}) %copy-start.2) | copy-done | bytes 792
  3.7 32.4 %shard_map.46 = bf16[256,192]{1,0:T(8,128)(2,1)S(1)} custom-call(bf16[1024,2048]{1,0:T(8,128)(2,1)S(1)} %copy-done, bf16[16,2048]{1,0:T(8,128)(2,1)S(1)} %copy-done.1, bf16[2048,2048]{1,0:T(8,128)(2,1)} %kinv_hbm.1, s32[1,192]{1,0:T(1,128)S(1)} %bitcast.1), custom_call_target="tpu_custom_call" | custom-call | flops 536870912 | bytes 8486912 | tf_op jit(solution)/shard_map/pallas_call | solution.py:207
  36.1 0.7 %copy.5 = bf16[256,192]{0,1:T(8,128)(2,1)} copy(bf16[256,192]{1,0:T(8,128)(2,1)S(1)} %shard_map.46) | data formatting | bytes 196608 | tf_op jit(solution)/shard_map/pallas_call | solution.py:207
Async XLA Ops:
  0.0 2.2 %copy-start = (bf16[1024,2048]{1,0:T(8,128)(2,1)S(1)}, bf16[1024,2048]{1,0:T(8,128)(2,1)}, u32[]{:S(2)}) copy-start(bf16[1024,2048]{1,0:T(8,128)(2,1)} %train_hbm.1) | copy-start | bytes 12582916
  2.2 0.8 %copy-start.1 = (bf16[16,2048]{1,0:T(8,128)(2,1)S(1)}, bf16[16,2048]{1,0:T(8,128)(2,1)}, u32[]{:S(2)}) copy-start(bf16[16,2048]{1,0:T(8,128)(2,1)} %pool_hbm.1) | copy-start | bytes 196612
  3.0 0.7 %copy-start.2 = (s32[192]{0:T(256)S(1)}, s32[192]{0:T(256)}, u32[]{:S(2)}) copy-start(s32[192]{0:T(256)} %param.7) | copy-start | bytes 2308

commit v2 on v1

--- a/solution.py
+++ b/solution.py
@@ -43,8 +43,8 @@
 
 def kernel(
     train_hbm, pool_hbm, kinv_hbm, ids_hbm, out_ref,
-    kinv, train, ids, pool, part1, got1, part2, got2, slices, precond, part3, got3, part4, got4,
-    load_sem, pool_send, pool_recv, send1, recv1, send2, recv2, send3, recv3, send4, recv4, send5, recv5, send6, recv6,
+    kinv, train, ids, pool, part1, got1, part2, got2, mine, precond, part3, got3, part4, got4,
+    load_sem, pool_send, pool_recv, send1, recv1, send2, recv2, send3, recv3, send4, recv4, send5, recv5,
 ):
     g, d, f = lax.axis_index("groups"), lax.axis_index("dp"), lax.axis_index("feat")
     x, c = f // 2, f % 2
@@ -52,7 +52,7 @@
     pool_rows = pool.shape[0] * pool.shape[1]
     sibling = (g, d, 2 * x + 1 - c)
     around = [(1 - g, 1 - x), (1 - g, x), (g, 1 - x), (g, x)]
-    me = c * 4 + g * 2 + x
+    held = train.shape[2]
 
     def remote(src, dst, send, recv, device):
         return pltpu.make_async_remote_copy(
@@ -74,10 +74,14 @@
     for i in range(8):
         core = 1 - c if i < 4 else c
         gg, xx = around[i % 4]
-        col = pl.multiple_of((core * 4 + gg * 2 + xx) * width, width)
+        col = pl.multiple_of((gg * 4 + 2 * xx + core) * width, width)
         kinv_loads.append(load(kinv_hbm.at[pl.ds(depth_from, depth), pl.ds(col, width)], kinv.at[i]))
     train_loads = [
-        load(train_hbm.at[pl.ds(i * train.shape[1], train.shape[1]), :], train.at[i]) for i in range(4)
+        load(
+            train_hbm.at[pl.ds(i * train.shape[1], train.shape[1]), pl.ds(pl.multiple_of(g * held, held), held)],
+            train.at[i],
+        )
+        for i in range(4)
     ]
     ids_load = load(ids_hbm, ids)
 
@@ -87,9 +91,16 @@
     for r in range(4):
         for gg in (g, 1 - g) if r else (1 - g,):
             pl.semaphore_signal(barrier, inc=1, device_id=(gg, d, (f + r) % 4), device_id_type=MESH)
-    pl.semaphore_wait(barrier, 10)
-
-    sends = []
+
+    @pl.when(f != d)
+    def _():
+        for r in range(1, 4):
+            pl.semaphore_signal(barrier, inc=1, device_id=(g, f, (f + r) % 4), device_id_type=MESH)
+        pl.semaphore_wait(barrier, 13)
+
+    @pl.when(f == d)
+    def _():
+        pl.semaphore_wait(barrier, 10)
 
     pool_copies = []
     for r in range(1, 4):
@@ -123,77 +134,66 @@
     for i in (2, 1, 0):
         copies2[i].wait_recv()
         total = total + got2[i]
-    slices[d] = total.astype(BF16)
-
+    mine[...] = total.astype(BF16)
+
+    here = pl.multiple_of(f * width, width)
     copies3 = []
-    for r in range(1, 4):
-        copy = remote(slices.at[d], slices.at[d], send3.at[r], recv3.at[r], (g, (d + r) % 4, f))
-        copy.start()
-        copies3.append(copy)
-
-    col = pl.multiple_of(me * width, width)
-
-    def forward(n, j):
-        mine = precond.at[:, pl.ds(col, width)]
-        across = remote(slices.at[j], mine, send4.at[n, 1], recv4.at[me], (1 - g, d, j))
-        beside = remote(slices.at[j], mine, send4.at[n, 0], recv4.at[me], (g, d, j))
-        across.start()
-
-        @pl.when(f != j)
-        def _():
-            beside.start()
-
-        @pl.when(f == j)
-        def _():
-            precond[:, pl.ds(col, width)] = slices[j]
-
-        return across, beside, j
-
-    forwards = [forward(0, d)]
-    for r in range(1, 4):
-        copies3[r - 1].wait_recv()
-        forwards.append(forward(r, (d - r + 4) % 4))
-    for r in range(1, 8):
-        k = (me + r) % 8
-        other = precond.at[:, pl.ds(pl.multiple_of(k * width, width), width)]
-        pltpu.make_async_remote_copy(
-            src_ref=other, dst_ref=other, send_sem=send4.at[0, 0], recv_sem=recv4.at[k],
-            device_id=sibling, device_id_type=MESH,
-        ).wait_recv()
+    for r in range(4):
+        target = (g, (d + r) % 4, d)
+        copies3.append(remote(mine, precond.at[:, pl.ds(here, width)], send3.at[r], recv3.at[f], target))
+    for r in (2, 1, 3):
+        copies3[r].start()
+
+    @pl.when(f != d)
+    def _():
+        copies3[0].start()
+
+    @pl.when(f == d)
+    def _():
+        precond[:, pl.ds(here, width)] = mine[...]
 
     for copy in train_loads:
         copy.wait()
+    ids_load.wait()
+    for r in range(4):
+        source = (f + r) % 4
+        place = precond.at[:, pl.ds(pl.multiple_of(source * width, width), width)]
+        arrival = remote(mine, place, send3.at[0], recv3.at[source], sibling)
+        if r:
+            arrival.wait_recv()
+        else:
+            pl.when(f != d)(arrival.wait_recv)
+
     left = precond[...]
 
     def term(j):
         return lax.dot_general(left, train[j], NT, preferred_element_type=F32)
 
-    copies5 = []
+    copies4 = []
     for i, xx in enumerate((1 - x, x)):
         part3[i] = term(2 * xx + 1 - c)
-        copy = remote(part3.at[i], got3.at[i], send5.at[i], recv5.at[i], sibling)
-        copy.start()
-        copies5.append(copy)
-    first = term(2 * (1 - x) + c)
-    copies5[0].wait_recv()
-    part4[...] = first + got3[0]
-    copy6 = remote(part4, got4, send6, recv6, (g, d, 2 * (1 - x) + c))
-    copy6.start()
-    second = term(f)
-    copies5[1].wait_recv()
-    second = second + got3[1]
-    ids_load.wait()
-    copy6.wait_recv()
-    out_ref[...] = pick_columns(second + got4[...], ids[...], pool_rows)
-
-    for copy in pool_copies + copies1 + copies2 + copies3 + copies5 + [copy6]:
+        copy = remote(part3.at[i], got3.at[i], send4.at[i], recv4.at[i], sibling)
+        copy.start()
+        copies4.append(copy)
+    terms = [term(2 * xx + c) for xx in (1 - x, x)]
+    copies5 = []
+    for i in range(2):
+        copies4[i].wait_recv()
+        part4[i] = terms[i] + got3[i]
+        for gg, xx in around[:1] + around[2:3] if i == 0 else around[1:2]:
+            n = len(copies5)
+            copy = remote(part4.at[i], got4.at[n], send5.at[n], recv5.at[n], (gg, d, 2 * xx + c))
+            copy.start()
+            copies5.append(copy)
+    total = part4[1]
+    for n in (2, 1, 0):
+        copies5[n].wait_recv()
+        total = total + got4[n]
+    out_ref[...] = pick_columns(total, ids[...], pool_rows)
+
+    for copy in pool_copies + copies1 + copies2 + copies3[1:] + copies4 + copies5:
         copy.wait_send()
-    for across, beside, j in forwards:
-        across.wait_send()
-
-        @pl.when(f != j)
-        def _(beside=beside):
-            beside.wait_send()
+    pl.when(f != d)(copies3[0].wait_send)
 
 
 def fused(train_feats, pool_feats, kernel_inv, test_ids):
@@ -204,6 +204,7 @@
     out_rows = rows // 4
     queries = test_ids.shape[0]
     dma = pltpu.SemaphoreType.DMA
+    held_in_hbm = (train_feats, pool_feats, kernel_inv, test_ids.reshape(1, queries))
     return pl.pallas_call(
         kernel,
         out_shape=jax.ShapeDtypeStruct((out_rows, queries), BF16),
@@ -211,31 +212,31 @@
         out_specs=pl.BlockSpec(memory_space=pltpu.VMEM),
         scratch_shapes=[
             pltpu.VMEM((8, depth, width), BF16),
-            pltpu.VMEM((4, out_rows, feats), BF16),
+            pltpu.VMEM((4, out_rows, depth), BF16),
             pltpu.VMEM((1, queries), jnp.int32),
             pltpu.VMEM((4, pool_block, depth), BF16),
             pltpu.VMEM((4, pool_rows, width), F32),
             pltpu.VMEM((4, pool_rows, width), F32),
             pltpu.VMEM((4, pool_rows, width), F32),
             pltpu.VMEM((3, pool_rows, width), F32),
-            pltpu.VMEM((4, pool_rows, width), BF16),
-            pltpu.VMEM((pool_rows, 8 * width), BF16),
+            pltpu.VMEM((pool_rows, width), BF16),
+            pltpu.VMEM((pool_rows, 4 * width), BF16),
             pltpu.VMEM((2, pool_rows, out_rows), F32),
             pltpu.VMEM((2, pool_rows, out_rows), F32),
-            pltpu.VMEM((pool_rows, out_rows), F32),
-            pltpu.VMEM((pool_rows, out_rows), F32),
+            pltpu.VMEM((2, pool_rows, out_rows), F32),
+            pltpu.VMEM((3, pool_rows, out_rows), F32),
             dma((14,)), dma((4,)), dma((4,)), dma((4,)), dma((4,)), dma((3,)), dma((3,)),
-            dma((4,)), dma((4,)), dma((4, 2)), dma((8,)), dma((2,)), dma((2,)), dma, dma,
+            dma((4,)), dma((4,)), dma((2,)), dma((2,)), dma((3,)), dma((3,)),
         ],
         compiler_params=pltpu.CompilerParams(
             collective_id=0, has_side_effects=True, vmem_limit_bytes=48 * 1024 * 1024
         ),
         cost_estimate=pl.CostEstimate(
-            flops=2 * pool_rows * feats * (kernel_inv.shape[1] // 2 + rows),
-            bytes_accessed=2 * (train_feats.size + kernel_inv.size // 2 + out_rows * queries),
+            flops=2 * pool_rows * feats * (kernel_inv.shape[1] + rows) // 2,
+            bytes_accessed=train_feats.size + kernel_inv.size + 2 * out_rows * queries,
             transcendentals=0,
         ),
-    )(train_feats, pool_feats, kernel_inv, test_ids.reshape(1, queries))
+    )(*[pltpu.with_memory_space_constraint(held, pltpu.HBM) for held in held_in_hbm])
 
 
 def solution(mesh):

time: 37 us -> 29.9 us (0.81)
  local copies, waits for them, and re-layouts: 4.45 us -> 0.75 us
  Pallas kernels: 32.4 us -> 29 us
    unnamed x6 -> x0, local copies, waits for them, and re-layouts: 3.7 us -> none
    pallas_call x1, Pallas kernels: 32.4 us -> 29 us  [fused(): pl.pallas_call(kernel, out_shape=jax.ShapeDtypeStruct((out_rows, queries)...]
where the time goes in v2:
time: 29.9 us; the launch traced here: 29.7 us
  Pallas kernels  29 us (97%)
  local copies, waits for them, and re-layouts  0.75 us (3%)
    pallas_call x1, Pallas kernels, fused(): pl.pallas_call(kernel, out_shape=jax.ShapeDtypeStruct((out_rows, queries)...  29 us
    pallas_call x1, local copies, waits for them, and re-layouts, fused(): pl.pallas_call(kernel, out_shape=jax.ShapeDtypeStruct((out_rows, queries)...  0.75 us

profile of v2, /device:TPU:0, one launch (start us, length us, event | category | flops | bytes accessed | tf_op | source)
XLA Modules:
  0.0 29.7 jit_solution(1962961012513347432)
XLA Ops:
  0.0 29.0 %shard_map.46 = bf16[256,192]{1,0:T(8,128)(2,1)S(1)} custom-call(bf16[1024,2048]{1,0:T(8,128)(2,1)} %train_hbm.1, bf16[16,2048]{1,0:T(8,128)(2,1)} %pool_hbm.1, bf16[2048,2048]{1,0:T(8,128)(2,1)} %kinv_hbm.1, s32[1,192]{1,0:T(1,128)} %bitcast.1), custom_call_target="tpu_custom_call" | custom-call | flops 402653184 | bytes 6389760 | tf_op jit(solution)/shard_map/pallas_call | solution.py:208
  29.0 0.7 %copy.5 = bf16[256,192]{0,1:T(8,128)(2,1)} copy(bf16[256,192]{1,0:T(8,128)(2,1)S(1)} %shard_map.46) | data formatting | bytes 196608 | tf_op jit(solution)/shard_map/pallas_call | solution.py:208

commit v3 on v2

--- a/solution.py
+++ b/solution.py
@@ -91,25 +91,19 @@
     for r in range(4):
         for gg in (g, 1 - g) if r else (1 - g,):
             pl.semaphore_signal(barrier, inc=1, device_id=(gg, d, (f + r) % 4), device_id_type=MESH)
-
-    @pl.when(f != d)
-    def _():
-        for r in range(1, 4):
-            pl.semaphore_signal(barrier, inc=1, device_id=(g, f, (f + r) % 4), device_id_type=MESH)
-        pl.semaphore_wait(barrier, 13)
-
-    @pl.when(f == d)
-    def _():
-        pl.semaphore_wait(barrier, 10)
-
+    pl.semaphore_wait(barrier, 10)
+
+    own_pool.wait()
+    outward = 1 - 2 * (d // 2)
     pool_copies = []
-    for r in range(1, 4):
-        copy = remote(pool_half, pool.at[d], pool_send.at[r], pool_recv.at[r], (g, (d + r) % 4, f))
+    for r in (3, 2, 1):
+        target = (g, (d + 4 + outward * r) % 4, f)
+        copy = remote(pool.at[d], pool.at[d], pool_send.at[r], pool_recv.at[d], target)
         copy.start()
         pool_copies.append(copy)
-    own_pool.wait()
-    for copy in pool_copies:
-        copy.wait_recv()
+    for r in (1, 2, 3):
+        source = (d + r) % 4
+        remote(pool.at[source], pool.at[source], pool_send.at[r], pool_recv.at[source], sibling).wait_recv()
     rows = pool[...].reshape(pool_rows, depth)
 
     copies1 = []
@@ -124,16 +118,19 @@
         kinv_loads[4 + i].wait()
         term = jnp.dot(rows, kinv[4 + i], preferred_element_type=F32)
         copies1[i].wait_recv()
-        part2[i] = term + got1[i]
+        both = term + got1[i]
+        if i == 3:
+            total = both
+        else:
+            part2[i] = both.astype(BF16)
         if i < 3:
             gg, xx = around[i]
             copy = remote(part2.at[i], got2.at[i], send2.at[i], recv2.at[i], (gg, d, 2 * xx + c))
             copy.start()
             copies2.append(copy)
-    total = part2[3]
     for i in (2, 1, 0):
         copies2[i].wait_recv()
-        total = total + got2[i]
+        total = total + got2[i].astype(F32)
     mine[...] = total.astype(BF16)
 
     here = pl.multiple_of(f * width, width)
@@ -155,6 +152,7 @@
     for copy in train_loads:
         copy.wait()
     ids_load.wait()
+
     for r in range(4):
         source = (f + r) % 4
         place = precond.at[:, pl.ds(pl.multiple_of(source * width, width), width)]
@@ -179,16 +177,17 @@
     copies5 = []
     for i in range(2):
         copies4[i].wait_recv()
-        part4[i] = terms[i] + got3[i]
+        both = terms[i] + got3[i]
+        part4[i] = both.astype(BF16)
         for gg, xx in around[:1] + around[2:3] if i == 0 else around[1:2]:
             n = len(copies5)
             copy = remote(part4.at[i], got4.at[n], send5.at[n], recv5.at[n], (gg, d, 2 * xx + c))
             copy.start()
             copies5.append(copy)
-    total = part4[1]
+    total = both
     for n in (2, 1, 0):
         copies5[n].wait_recv()
-        total = total + got4[n]
+        total = total + got4[n].astype(F32)
     out_ref[...] = pick_columns(total, ids[...], pool_rows)
 
     for copy in pool_copies + copies1 + copies2 + copies3[1:] + copies4 + copies5:
@@ -217,14 +216,14 @@
             pltpu.VMEM((4, pool_block, depth), BF16),
             pltpu.VMEM((4, pool_rows, width), F32),
             pltpu.VMEM((4, pool_rows, width), F32),
-            pltpu.VMEM((4, pool_rows, width), F32),
-            pltpu.VMEM((3, pool_rows, width), F32),
+            pltpu.VMEM((4, pool_rows, width), BF16),
+            pltpu.VMEM((3, pool_rows, width), BF16),
             pltpu.VMEM((pool_rows, width), BF16),
             pltpu.VMEM((pool_rows, 4 * width), BF16),
+            pltpu.VMEM((4, pool_rows, out_rows), F32),
             pltpu.VMEM((2, pool_rows, out_rows), F32),
-            pltpu.VMEM((2, pool_rows, out_rows), F32),
-            pltpu.VMEM((2, pool_rows, out_rows), F32),
-            pltpu.VMEM((3, pool_rows, out_rows), F32),
+            pltpu.VMEM((2, pool_rows, out_rows), BF16),
+            pltpu.VMEM((3, pool_rows, out_rows), BF16),
             dma((14,)), dma((4,)), dma((4,)), dma((4,)), dma((4,)), dma((3,)), dma((3,)),
             dma((4,)), dma((4,)), dma((2,)), dma((2,)), dma((3,)), dma((3,)),
         ],

time: 29.9 us -> 26.8 us (0.90)
  Pallas kernels: 29 us -> 25.9 us
    pallas_call x1, Pallas kernels: 29 us -> 25.9 us  [fused(): pl.pallas_call(kernel, out_shape=jax.ShapeDtypeStruct((out_rows, queries)...]
where the time goes in v3:
time: 26.8 us; the launch traced here: 26.7 us
  Pallas kernels  25.9 us (97%)
  local copies, waits for them, and re-layouts  0.75 us (3%)
    pallas_call x1, Pallas kernels, fused(): pl.pallas_call(kernel, out_shape=jax.ShapeDtypeStruct((out_rows, queries)...  25.9 us
    pallas_call x1, local copies, waits for them, and re-layouts, fused(): pl.pallas_call(kernel, out_shape=jax.ShapeDtypeStruct((out_rows, queries)...  0.75 us

profile of v3, /device:TPU:0, one launch (start us, length us, event | category | flops | bytes accessed | tf_op | source)
XLA Modules:
  0.0 26.7 jit_solution(9922376507802110216)
XLA Ops:
  0.0 25.9 %shard_map.46 = bf16[256,192]{1,0:T(8,128)(2,1)S(1)} custom-call(bf16[1024,2048]{1,0:T(8,128)(2,1)} %train_hbm.1, bf16[16,2048]{1,0:T(8,128)(2,1)} %pool_hbm.1, bf16[2048,2048]{1,0:T(8,128)(2,1)} %kinv_hbm.1, s32[1,192]{1,0:T(1,128)} %bitcast.1), custom_call_target="tpu_custom_call" | custom-call | flops 402653184 | bytes 6389760 | tf_op jit(solution)/shard_map/pallas_call | solution.py:207
  26.0 0.7 %copy.5 = bf16[256,192]{0,1:T(8,128)(2,1)} copy(bf16[256,192]{1,0:T(8,128)(2,1)S(1)} %shard_map.46) | data formatting | bytes 196608 | tf_op jit(solution)/shard_map/pallas_call | solution.py:207

commit v4 on v3

--- a/solution.py
+++ b/solution.py
@@ -43,7 +43,7 @@
 
 def kernel(
     train_hbm, pool_hbm, kinv_hbm, ids_hbm, out_ref,
-    kinv, train, ids, pool, part1, got1, part2, got2, mine, precond, part3, got3, part4, got4,
+    kinv, train, turned, ids, pool, part1, got1, part2, got2, mine, precond, part3, got3, part4, got4,
     load_sem, pool_send, pool_recv, send1, recv1, send2, recv2, send3, recv3, send4, recv4, send5, recv5,
 ):
     g, d, f = lax.axis_index("groups"), lax.axis_index("dp"), lax.axis_index("feat")
@@ -70,12 +70,13 @@
     depth_from = pl.multiple_of(g * depth, depth)
     pool_half = pool_hbm.at[:, pl.ds(depth_from, depth)]
     own_pool = load(pool_half, pool.at[d])
-    kinv_loads = []
-    for i in range(8):
-        core = 1 - c if i < 4 else c
-        gg, xx = around[i % 4]
-        col = pl.multiple_of((gg * 4 + 2 * xx + core) * width, width)
-        kinv_loads.append(load(kinv_hbm.at[pl.ds(depth_from, depth), pl.ds(col, width)], kinv.at[i]))
+    barrier = pltpu.get_barrier_semaphore()
+    for r in range(1, 4):
+        pl.semaphore_signal(barrier, inc=1, device_id=(g, (d + r) % 4, f), device_id_type=MESH)
+    for r in range(4):
+        for gg in (g, 1 - g) if r else (1 - g,):
+            pl.semaphore_signal(barrier, inc=1, device_id=(gg, d, (f + r) % 4), device_id_type=MESH)
+
     train_loads = [
         load(
             train_hbm.at[pl.ds(i * train.shape[1], train.shape[1]), pl.ds(pl.multiple_of(g * held, held), held)],
@@ -83,14 +84,14 @@
         )
         for i in range(4)
     ]
+    kinv_loads = []
+    for i in range(8):
+        core = 1 - c if i < 4 else c
+        gg, xx = around[i % 4]
+        col = pl.multiple_of((gg * 4 + 2 * xx + core) * width, width)
+        kinv_loads.append(load(kinv_hbm.at[pl.ds(depth_from, depth), pl.ds(col, width)], kinv.at[i]))
     ids_load = load(ids_hbm, ids)
 
-    barrier = pltpu.get_barrier_semaphore()
-    for r in range(1, 4):
-        pl.semaphore_signal(barrier, inc=1, device_id=(g, (d + r) % 4, f), device_id_type=MESH)
-    for r in range(4):
-        for gg in (g, 1 - g) if r else (1 - g,):
-            pl.semaphore_signal(barrier, inc=1, device_id=(gg, d, (f + r) % 4), device_id_type=MESH)
     pl.semaphore_wait(barrier, 10)
 
     own_pool.wait()
@@ -101,6 +102,9 @@
         copy = remote(pool.at[d], pool.at[d], pool_send.at[r], pool_recv.at[d], target)
         copy.start()
         pool_copies.append(copy)
+    for i in range(4):
+        train_loads[i].wait()
+        turned[i] = train[i].T
     for r in (1, 2, 3):
         source = (d + r) % 4
         remote(pool.at[source], pool.at[source], pool_send.at[r], pool_recv.at[source], sibling).wait_recv()
@@ -136,9 +140,9 @@
     here = pl.multiple_of(f * width, width)
     copies3 = []
     for r in range(4):
-        target = (g, (d + r) % 4, d)
+        target = (g, (d + 4 + outward * r) % 4, d)
         copies3.append(remote(mine, precond.at[:, pl.ds(here, width)], send3.at[r], recv3.at[f], target))
-    for r in (2, 1, 3):
+    for r in (3, 2, 1):
         copies3[r].start()
 
     @pl.when(f != d)
@@ -149,35 +153,31 @@
     def _():
         precond[:, pl.ds(here, width)] = mine[...]
 
-    for copy in train_loads:
-        copy.wait()
     ids_load.wait()
 
-    for r in range(4):
-        source = (f + r) % 4
-        place = precond.at[:, pl.ds(pl.multiple_of(source * width, width), width)]
-        arrival = remote(mine, place, send3.at[0], recv3.at[source], sibling)
+    chunks = [2 * xx + cc for cc in (1 - c, c) for xx in (1 - x, x)]
+    copies4 = []
+    for r, source in enumerate((f, 2 * x + 1 - c, 2 * (1 - x) + c, 2 * (1 - x) + 1 - c)):
+        columns = pl.ds(pl.multiple_of(source * width, width), width)
+        arrival = remote(mine, precond.at[:, columns], send3.at[0], recv3.at[source], sibling)
         if r:
             arrival.wait_recv()
         else:
             pl.when(f != d)(arrival.wait_recv)
-
-    left = precond[...]
-
-    def term(j):
-        return lax.dot_general(left, train[j], NT, preferred_element_type=F32)
-
-    copies4 = []
-    for i, xx in enumerate((1 - x, x)):
-        part3[i] = term(2 * xx + 1 - c)
-        copy = remote(part3.at[i], got3.at[i], send4.at[i], recv4.at[i], sibling)
-        copy.start()
-        copies4.append(copy)
-    terms = [term(2 * xx + c) for xx in (1 - x, x)]
+        left = precond[:, columns]
+        for i, chunk in enumerate(chunks):
+            more = jnp.dot(left, turned[chunk, columns, :], preferred_element_type=F32)
+            if r == 0:
+                part3[i] = more
+            else:
+                part3[i] = part3[i] + more
+            if r == 3 and i < 2:
+                copies4.append(remote(part3.at[i], got3.at[i], send4.at[i], recv4.at[i], sibling))
+                copies4[i].start()
     copies5 = []
     for i in range(2):
         copies4[i].wait_recv()
-        both = terms[i] + got3[i]
+        both = part3[2 + i] + got3[i]
         part4[i] = both.astype(BF16)
         for gg, xx in around[:1] + around[2:3] if i == 0 else around[1:2]:
             n = len(copies5)
@@ -212,6 +212,7 @@
         scratch_shapes=[
             pltpu.VMEM((8, depth, width), BF16),
             pltpu.VMEM((4, out_rows, depth), BF16),
+            pltpu.VMEM((4, depth, out_rows), BF16),
             pltpu.VMEM((1, queries), jnp.int32),
             pltpu.VMEM((4, pool_block, depth), BF16),
             pltpu.VMEM((4, pool_rows, width), F32),
@@ -221,7 +222,7 @@
             pltpu.VMEM((pool_rows, width), BF16),
             pltpu.VMEM((pool_rows, 4 * width), BF16),
             pltpu.VMEM((4, pool_rows, out_rows), F32),
-            pltpu.VMEM((2, pool_rows, out_rows), F32),
+            pltpu.VMEM((4, pool_rows, out_rows), F32),
             pltpu.VMEM((2, pool_rows, out_rows), BF16),
             pltpu.VMEM((3, pool_rows, out_rows), BF16),
             dma((14,)), dma((4,)), dma((4,)), dma((4,)), dma((4,)), dma((3,)), dma((3,)),

time: 26.8 us -> 26.3 us (0.981)
  Pallas kernels: 25.9 us -> 25.4 us
    pallas_call x1, Pallas kernels: 25.9 us -> 25.4 us  [fused(): pl.pallas_call(kernel, out_shape=jax.ShapeDtypeStruct((out_rows, queries)...]
where the time goes in v4:
time: 26.3 us; the launch traced here: 26.1 us
  Pallas kernels  25.4 us (97%)
  local copies, waits for them, and re-layouts  0.75 us (3%)
    pallas_call x1, Pallas kernels, fused(): pl.pallas_call(kernel, out_shape=jax.ShapeDtypeStruct((out_rows, queries)...  25.4 us
    pallas_call x1, local copies, waits for them, and re-layouts, fused(): pl.pallas_call(kernel, out_shape=jax.ShapeDtypeStruct((out_rows, queries)...  0.75 us

profile of v4, /device:TPU:0, one launch (start us, length us, event | category | flops | bytes accessed | tf_op | source)
XLA Modules:
  0.0 26.1 jit_solution(4341812154207019249)
XLA Ops:
  0.0 25.4 %shard_map.46 = bf16[256,192]{1,0:T(8,128)(2,1)S(1)} custom-call(bf16[1024,2048]{1,0:T(8,128)(2,1)} %train_hbm.1, bf16[16,2048]{1,0:T(8,128)(2,1)} %pool_hbm.1, bf16[2048,2048]{1,0:T(8,128)(2,1)} %kinv_hbm.1, s32[1,192]{1,0:T(1,128)} %bitcast.1), custom_call_target="tpu_custom_call" | custom-call | flops 402653184 | bytes 6389760 | tf_op jit(solution)/shard_map/pallas_call | solution.py:207
  25.4 0.7 %copy.5 = bf16[256,192]{0,1:T(8,128)(2,1)} copy(bf16[256,192]{1,0:T(8,128)(2,1)S(1)} %shard_map.46) | data formatting | bytes 196608 | tf_op jit(solution)/shard_map/pallas_call | solution.py:207
